TPU v7x, 128 devices: a whole 4x4x4 slice. The times are simulated.
128 devices in a mesh: prow: 8 (over x, core), pcol: 16 (over z, y).
Axes of the slice: x: 4, y: 4, z: 4, core: 2. Of those that a mesh axis runs over, the one named last changes fastest.
Arguments:
- matrix: float32 [8, 16, 768, 384], P('prow', 'pcol'), may hold values from -6 to 6
- pivots: int32 [3, 384], replicated, may hold values from 0 to 6143, as said below
- lower_inv: float32 [3, 384, 384], replicated, may hold values from -0.3125 to 0.3125
- upper_inv: float32 [3, 384, 384], replicated, may hold values from -0.015625 to 0.015625
Outputs:
- factored: float32 [8, 16, 768, 384], P('prow', 'pcol')
Inputs may be any that keep to these rules, and one draw needn't show every extreme that they name: Within one step s the indices pivots[s, i] are distinct, and each equals s * 384 + i or lies between (s + 1) * 384 and 6143.
All inputs are finite; a program needn't handle non-finite values.
Results may differ from a plain program's by a relative error of at most 0.0002.
Values sent between devices are 32-bit elements; how exact they have to be, the bound alone decides.
No kernel may reach another device: no remote copies, remote signals or barrier semaphores. Data moves between devices by JAX's collectives and lax.ppermute only.
A program may use at most 64 MiB of HBM per device.

v0:
```python
import jax
import jax.numpy as jnp
from jax import lax
from jax.sharding import PartitionSpec as P

PRECISE = lax.Precision.HIGHEST


def over_pieces(x, axis):
    parts = lax.all_gather(x, axis)
    return parts.sum(axis=0)


def spread(value, axis, source):
    kept = jnp.where(lax.axis_index(axis) == source, value, 0).astype(value.dtype)
    return lax.psum(kept, axis)


def on_device(matrix, pivots, lower_inv, upper_inv):
    prow_count = lax.axis_size("prow")
    pcol_count = lax.axis_size("pcol")
    prow_index = lax.axis_index("prow")
    pcol_index = lax.axis_index("pcol")
    local_tile = matrix[0, 0]
    local_rows, local_cols = local_tile.shape
    width = lower_inv.shape[1]
    row_ids = jnp.arange(local_rows, dtype=jnp.int32)
    global_rows = (row_ids // width * prow_count + prow_index) * width + row_ids % width
    col_ids = jnp.arange(local_cols, dtype=jnp.int32)
    global_cols = (col_ids // width * pcol_count + pcol_index) * width + col_ids % width
    offsets = jnp.arange(width, dtype=jnp.int32)
    for section in range(pivots.shape[0]):
        start = section * width
        finish = start + width
        pivot_list = pivots[section]
        block_targets = start + offsets
        owner_row = section % prow_count
        owner_col = section % pcol_count
        row_start = section // prow_count * width
        targets = jnp.concatenate([block_targets, pivot_list])
        sources = jnp.concatenate([pivot_list, block_targets])
        source_owned = sources // width % prow_count == prow_index
        source_local = jnp.where(
            source_owned, sources // width // prow_count * width + sources % width, 0
        )
        picked = jnp.where(source_owned[:, None], local_tile[source_local], 0.0)
        arrived = over_pieces(picked, "prow")
        target_owned = targets // width % prow_count == prow_index
        target_local = jnp.where(
            target_owned, targets // width // prow_count * width + targets % width, local_rows
        )
        local_tile = local_tile.at[target_local].set(arrived, mode="drop")
        pivot_rows = arrived[:width]
        lower_unit = jnp.eye(width, dtype=jnp.float32) + jnp.tril(lower_inv[section], -1)
        upper_tri = jnp.triu(upper_inv[section])
        col_mask = (global_cols >= finish)[None, :]
        row_mask = (global_rows >= finish)[:, None]
        product = jnp.dot(
            lower_unit, pivot_rows, precision=PRECISE, preferred_element_type=jnp.float32
        )
        upper_rows = jnp.where(col_mask, product, 0.0)
        current = local_tile[row_start : row_start + width]
        stored = jnp.where(col_mask & (prow_index == owner_row), upper_rows, current)
        local_tile = local_tile.at[row_start : row_start + width].set(stored)
        col_start = section // pcol_count * width
        panel = local_tile

        def lower_product(source_panel):
            product = jnp.dot(
                source_panel, upper_tri, precision=PRECISE, preferred_element_type=jnp.float32
            )
            return jnp.where(row_mask, product, 0.0)

        def owned_lower():
            return lower_product(panel)

        def empty_panel():
            return jnp.zeros_like(panel)

        owned_panel = lax.cond(pcol_index == owner_col, owned_lower, empty_panel)
        lower_panel = spread(owned_panel, "pcol", owner_col)
        kept = jnp.where(row_mask & (pcol_index == owner_col), lower_panel, panel)
        local_tile = local_tile.at[:, col_start : col_start + width].set(kept)
        update = jnp.dot(
            lower_panel, upper_rows, precision=PRECISE, preferred_element_type=jnp.float32
        )
        local_tile = local_tile - update
    return local_tile[None, None]


def solution(mesh):
    return jax.shard_map(
        on_device,
        mesh=mesh,
        in_specs=(P("prow", "pcol", None, None), P(), P(), P()),
        out_specs=P("prow", "pcol", None, None),
        check_vma=False,
    )
```

profile of v0, /device:TPU:0, one launch (start us, length us, event | category | flops | bytes accessed | tf_op | source)
XLA Modules:
  0.0 510.7 jit_solution(8348842341577072828)
XLA Ops:
  6.5 0.0 all-gather.4.cloned.1.call-start
  6.5 1.3 copy.37
  7.8 0.0 copy-done.8
  7.8 0.6 slice_reduce_fusion
  8.4 0.1 fusion.56
  8.6 2.1 gather_fusion
  10.7 1.2 bitcast_select_fusion.8
  11.9 0.0 all-gather.4.cloned.1.call-update
  11.9 0.0 all-reduce.4.cloned.1.call-start
  12.1 0.8 iota_compare_fusion.4
  12.9 55.8 %all-gather.4.cloned.1.call-done = f32[8,768,384]{2,1,0:T(8,128)} async-done(((f32[1,768,384]{2,1,0:T(8,128)}), f32[8,768,384]{2,1,0:T(8,128)}) %all-gather.4.cloned.1.call-update) | async-done | bytes 9437200 | tf_op jit(solution)/shard_map/all_gather | solution.py:10
  68.7 4.3 reduce_sum.27
  72.9 5.7 %scatter_fusion = f32[768,384]{1,0:T(8,128)S(1)} fusion(f32[768,384]{1,0:T(8,128)S(1)} %bitcast.61, s32[768]{0:T(1024)S(1)} %get-tuple-element.181, f32[768,384]{1,0:T(8,128)S(1)} %reduce_sum.27), kind=kCustom, calls=%fused_computation.3 | custom fusion | bytes 3542016 | tf_op jit(solution)/shard_map/scatter | solution.py:52
  78.6 0.0 copy-start
  78.6 3.5 fusion.17
  82.2 0.0 copy-done
  82.2 4.4 conditional.3
  82.2 4.0 fusion
  86.2 0.4 copy.12
  86.6 1.1 broadcast_select_fusion.2
  87.7 0.0 all-reduce.4.cloned.1.call-update
  87.7 0.2 all-gather.6.cloned.1.call-start
  88.0 0.4 copy-done.7
  88.4 0.1 fusion.58
  88.5 82.4 %all-reduce.4.cloned.1.call-done = f32[768,384]{1,0:T(8,128)} async-done(((f32[768,384]{1,0:T(8,128)}), f32[768,384]{1,0:T(8,128)}) %all-reduce.4.cloned.1.call-update) | async-done | bytes 1179664 | tf_op jit(solution)/shard_map/psum | solution.py:16
  170.8 0.0 copy-done.3
  170.8 4.0 convolution_subtract_fusion.2
  174.8 2.1 gather_fusion.1
  176.9 1.2 bitcast_select_fusion.7
  178.1 0.0 all-gather.6.cloned.1.call-update
  178.2 0.0 all-reduce.6.cloned.1.call-start
  178.2 53.3 %all-gather.6.cloned.1.call-done = f32[8,768,384]{2,1,0:T(8,128)} async-done(((f32[1,768,384]{2,1,0:T(8,128)}), f32[8,768,384]{2,1,0:T(8,128)}) %all-gather.6.cloned.1.call-update) | async-done | bytes 9437200 | tf_op jit(solution)/shard_map/all_gather | solution.py:10
  231.5 4.3 reduce_sum.28
  235.8 5.7 %scatter_fusion.1 = f32[768,384]{1,0:T(8,128)S(1)} fusion(f32[768,384]{1,0:T(8,128)S(1)} %convolution_subtract_fusion.2, s32[768]{0:T(1024)S(1)} %get-tuple-element.179, f32[768,384]{1,0:T(8,128)S(1)} %reduce_sum.28), kind=kCustom, calls=%fused_computation.4 | custom fusion | bytes 3542016 | tf_op jit(solution)/shard_map/scatter | solution.py:52
  241.5 0.0 copy-start.1
  241.5 3.5 fusion.15
  245.0 0.0 copy-done.1
  245.0 0.1 conditional.4
  245.0 0.1 broadcast.1739.clone
  245.1 1.1 broadcast_select_fusion.1
  246.2 0.0 all-reduce.6.cloned.1.call-update
  246.2 0.3 all-gather.8.cloned.1.call-start
  246.5 0.4 copy-done.6
  246.9 0.1 fusion.60
  247.0 86.9 %all-reduce.6.cloned.1.call-done = f32[768,384]{1,0:T(8,128)} async-done(((f32[768,384]{1,0:T(8,128)}), f32[768,384]{1,0:T(8,128)}) %all-reduce.6.cloned.1.call-update) | async-done | bytes 1179664 | tf_op jit(solution)/shard_map/psum | solution.py:16
  333.9 0.0 copy-done.4
  333.9 4.0 convolution_subtract_fusion.1
  337.9 2.1 gather_fusion.2
  340.0 1.2 bitcast_select_fusion.6
  341.2 0.0 all-gather.8.cloned.1.call-update
  341.3 0.0 all-reduce.8.cloned.1.call-start
  341.3 53.3 %all-gather.8.cloned.1.call-done = f32[8,768,384]{2,1,0:T(8,128)} async-done(((f32[1,768,384]{2,1,0:T(8,128)}), f32[8,768,384]{2,1,0:T(8,128)}) %all-gather.8.cloned.1.call-update) | async-done | bytes 9437200 | tf_op jit(solution)/shard_map/all_gather | solution.py:10
  394.6 4.3 reduce_sum.29
  398.9 5.7 %scatter_fusion.2 = f32[768,384]{1,0:T(8,128)S(1)} fusion(f32[768,384]{1,0:T(8,128)S(1)} %convolution_subtract_fusion.1, s32[768]{0:T(1024)S(1)} %get-tuple-element.177, f32[768,384]{1,0:T(8,128)S(1)} %reduce_sum.29), kind=kCustom, calls=%fused_computation.5 | custom fusion | bytes 3542016 | tf_op jit(solution)/shard_map/scatter | solution.py:52
  404.6 0.0 copy-start.2
  404.6 3.5 fusion.13
  408.1 0.0 copy-done.2
  408.1 0.3 conditional.5
  408.1 0.1 broadcast.1740.clone
  408.5 1.1 broadcast_select_fusion
  409.6 0.0 all-reduce.8.cloned.1.call-update
  409.6 89.2 %all-reduce.8.cloned.1.call-done = f32[768,384]{1,0:T(8,128)} async-done(((f32[768,384]{1,0:T(8,128)}), f32[768,384]{1,0:T(8,128)}) %all-reduce.8.cloned.1.call-update) | async-done | bytes 1179664 | tf_op jit(solution)/shard_map/psum | solution.py:16
  498.8 0.0 copy-done.5
  498.8 5.0 fusion.12
  (29 shorter events, 0.3 us)
Async XLA Ops:
  6.5 1.3 copy-start.8
  6.5 62.1 %all-gather.4.cloned.1.call-start = ((), (), s32[]{:S(2)}) async-start(), calls=%async_computation | async-start | bytes 10616832 | tf_op jit(solution)/shard_map/all_gather | solution.py:10
  11.9 158.9 %all-reduce.4.cloned.1.call-start = ((), (), s32[]{:S(2)}) async-start(), calls=%async_computation.1 | async-start | bytes 2359296 | tf_op jit(solution)/shard_map/psum | solution.py:16
  78.6 3.5 copy-start
  87.7 0.7 copy-start.7
  87.7 83.2 %copy-start.3 = (f32[384,384]{1,0:T(8,128)S(1)}, f32[384,384]{1,0:T(8,128)}, u32[]{:S(2)}) copy-start(f32[384,384]{1,0:T(8,128)} %get-tuple-element.186) | copy-start | bytes 1769476
  87.7 143.8 %all-gather.6.cloned.1.call-start = ((), (), s32[]{:S(2)}) async-start(), calls=%async_computation.2 | async-start | bytes 10616832 | tf_op jit(solution)/shard_map/all_gather | solution.py:10
  178.2 155.8 %all-reduce.6.cloned.1.call-start = ((), (), s32[]{:S(2)}) async-start(), calls=%async_computation.3 | async-start | bytes 2359296 | tf_op jit(solution)/shard_map/psum | solution.py:16
  241.5 3.5 copy-start.1
  246.2 0.7 copy-start.6
  246.2 87.8 %copy-start.4 = (f32[384,384]{1,0:T(8,128)S(1)}, f32[384,384]{1,0:T(8,128)}, u32[]{:S(2)}) copy-start(f32[384,384]{1,0:T(8,128)} %get-tuple-element.188) | copy-start | bytes 1769476
  246.2 148.4 %all-gather.8.cloned.1.call-start = ((), (), s32[]{:S(2)}) async-start(), calls=%async_computation.4 | async-start | bytes 10616832 | tf_op jit(solution)/shard_map/all_gather | solution.py:10
  341.3 157.6 %all-reduce.8.cloned.1.call-start = ((), (), s32[]{:S(2)}) async-start(), calls=%async_computation.5 | async-start | bytes 2359296 | tf_op jit(solution)/shard_map/psum | solution.py:16
  404.6 3.5 copy-start.2
  409.5 89.3 %copy-start.5 = (f32[384,384]{1,0:T(8,128)S(1)}, f32[384,384]{1,0:T(8,128)}, u32[]{:S(2)}) copy-start(f32[384,384]{1,0:T(8,128)} %get-tuple-element.190) | copy-start | bytes 1769476
Sparse Core Ops, SparseCore 0:
  12.1 56.5 all-gather.3
  87.8 82.9 all-reduce.3
  178.3 53.1 all-gather.5
  246.3 87.5 all-reduce.5
  341.4 53.1 all-gather.7
  409.7 89.0 all-reduce.7
where the time goes:
time: 511 us
  waiting for transfers between devices  421 us (82%)
  matrix products  27.5 us (5%)
  local copies, waits for them, and re-layouts  26.7 us (5%)
  other arithmetic  20.9 us (4%)
  between operations  13.8 us (3%)
    psum x3, waiting for transfers between devices, spread(): return lax.psum(kept, axis)  259 us
    all_gather x3, waiting for transfers between devices, over_pieces(): parts = lax.all_gather(x, axis)  162 us
    scatter x3, local copies, waits for them, and re-layouts, on_device(): local_tile = local_tile.at[target_local].set(arrived, mode='drop')  17.1 us
    dot_general x3, matrix products, on_device(): jnp.dot(lower_panel, upper_rows, precision=PRECISE, preferred_element_typ...  12.9 us
    reduce_sum x3, other arithmetic, over_pieces(): return parts.sum(axis=0)  12.8 us
    dot_general x3, matrix products, on_device(): jnp.dot(lower_unit, pivot_rows, precision=PRECISE, preferred_element_type...  10.5 us
  transfers between devices with their start and end apart: 6, of which 6 were waited for; matrix products, arithmetic and copies ran while one was open for 0% of the time, Pallas kernels for 0%

commit v1 on v0

--- a/solution.py
+++ b/solution.py
@@ -13,7 +13,7 @@
 
 def spread(value, axis, source):
     kept = jnp.where(lax.axis_index(axis) == source, value, 0).astype(value.dtype)
-    return lax.psum(kept, axis)
+    return jnp.sum(lax.all_gather(kept, axis), axis=0)
 
 
 def on_device(matrix, pivots, lower_inv, upper_inv):

time: 511 us -> 674 us (1.32); the launches traced: 511 us -> 666 us
  waiting for transfers between devices: 421 us -> 525 us
  local copies, waits for them, and re-layouts: 26.7 us -> 66.5 us
  other arithmetic: 20.9 us -> 32.1 us
    all_gather x0 -> x3, waiting for transfers between devices: none -> 361 us  [spread(): return jnp.sum(lax.all_gather(kept, axis), axis=0)]
    psum x3 -> x0, waiting for transfers between devices: 259 us -> none  [spread(): return lax.psum(kept, axis)]
    unnamed x19 -> x20, local copies, waits for them, and re-layouts: 2.07 us -> 38.2 us
    reduce_sum x0 -> x3, other arithmetic: none -> 9.63 us  [spread(): return jnp.sum(lax.all_gather(kept, axis), axis=0)]
where the time goes in v1:
time: 674 us; the launch traced here: 666 us
  waiting for transfers between devices  525 us (78%)
  local copies, waits for them, and re-layouts  66.5 us (10%)
  other arithmetic  32.1 us (5%)
  matrix products  26.5 us (4%)
  between operations  14.1 us (2%)
    all_gather x3, waiting for transfers between devices, spread(): return jnp.sum(lax.all_gather(kept, axis), axis=0)  361 us
    all_gather x3, waiting for transfers between devices, over_pieces(): parts = lax.all_gather(x, axis)  164 us
    unnamed x20, local copies, waits for them, and re-layouts  38.2 us
    scatter x3, local copies, waits for them, and re-layouts, on_device(): local_tile = local_tile.at[target_local].set(arrived, mode='drop')  17.3 us
  transfers between devices with their start and end apart: 6, of which 6 were waited for; matrix products, arithmetic and copies ran while one was open for 0% of the time, Pallas kernels for 0%

profile of v1, /device:TPU:0, one launch (start us, length us, event | category | flops | bytes accessed | tf_op | source)
XLA Modules:
  0.0 665.7 jit_solution(17857442303662967924)
XLA Ops:
  6.5 1.3 copy.28
  7.8 1.2 slice_reduce_fusion
  9.0 0.1 fusion.56
  9.1 2.1 gather_fusion
  11.3 1.2 bitcast_select_fusion.8
  12.5 0.0 all-gather.10.cloned.1.call-update
  12.5 0.0 all-gather.16.cloned.1.call-start
  12.6 0.1 fusion.58
  12.7 0.1 iota_compare_fusion.4
  12.9 56.3 %all-gather.10.cloned.1.call-done = f32[8,768,384]{2,1,0:T(8,128)} async-done(((f32[1,768,384]{2,1,0:T(8,128)}), f32[8,768,384]{2,1,0:T(8,128)}) %all-gather.10.cloned.1.call-update) | async-done | bytes 9437200 | tf_op jit(solution)/shard_map/all_gather | solution.py:10
  69.2 4.3 reduce_sum.54
  73.5 5.7 scatter_fusion
  79.2 3.4 fusion.17
  82.7 4.1 conditional.3
  82.7 4.0 fusion
  86.7 1.1 broadcast_select_fusion.2
  87.8 0.0 all-gather.16.cloned.1.call-update
  87.8 0.6 all-gather.12.cloned.1.call-start
  88.4 0.6 compare_and_fusion
  89.0 0.6 fusion.41
  89.6 116.8 %all-gather.16.cloned.1.call-done = f32[12288,384]{0,1:T(8,128)} async-done(((f32[768,384]{0,1:T(8,128)}), f32[12288,384]{0,1:T(8,128)}) %all-gather.16.cloned.1.call-update) | async-done | bytes 18874384 | tf_op jit(solution)/shard_map/all_gather | solution.py:16
  206.4 12.1 %copy.8 = f32[48,8,16,768]{3,2,1,0:T(8,128)S(1)} copy(f32[48,8,16,768]{3,1,2,0:T(8,128)} %bitcast.78) | data formatting | bytes 37748736
  218.6 3.2 bitcast_reduce_fusion.2
  221.8 1.4 copy.5
  223.2 3.8 convolution_subtract_fusion.2
  227.0 2.1 gather_fusion.1
  229.1 1.2 bitcast_select_fusion.7
  230.3 0.0 all-gather.12.cloned.1.call-update
  230.3 0.0 all-gather.18.cloned.1.call-start
  230.4 53.8 %all-gather.12.cloned.1.call-done = f32[8,768,384]{2,1,0:T(8,128)} async-done(((f32[1,768,384]{2,1,0:T(8,128)}), f32[8,768,384]{2,1,0:T(8,128)}) %all-gather.12.cloned.1.call-update) | async-done | bytes 9437200 | tf_op jit(solution)/shard_map/all_gather | solution.py:10
  284.2 4.3 reduce_sum.56
  288.5 5.7 scatter_fusion.1
  294.2 3.5 fusion.15
  297.7 0.3 conditional.4
  297.7 0.1 broadcast.1739
  297.9 1.1 broadcast_select_fusion.1
  299.0 0.0 all-gather.18.cloned.1.call-update
  299.1 0.0 all-gather.14.cloned.1.call-start
  299.1 0.6 copy-done.4
  299.7 0.1 fusion.60
  299.8 0.5 compare_and_fusion.1
  300.3 0.6 fusion.43
  300.9 120.7 %all-gather.18.cloned.1.call-done = f32[12288,384]{0,1:T(8,128)} async-done(((f32[768,384]{0,1:T(8,128)}), f32[12288,384]{0,1:T(8,128)}) %all-gather.18.cloned.1.call-update) | async-done | bytes 18874384 | tf_op jit(solution)/shard_map/all_gather | solution.py:16
  421.6 12.1 %copy.9 = f32[48,8,16,768]{3,2,1,0:T(8,128)S(1)} copy(f32[48,8,16,768]{3,1,2,0:T(8,128)} %bitcast.77) | data formatting | bytes 37748736
  433.7 3.2 bitcast_reduce_fusion.1
  436.9 1.4 copy.6
  438.3 3.8 convolution_subtract_fusion.1
  442.2 2.1 gather_fusion.2
  444.3 1.2 bitcast_select_fusion.6
  445.5 0.0 all-gather.14.cloned.1.call-update
  445.5 0.0 all-gather.20.cloned.1.call-start
  445.6 53.8 %all-gather.14.cloned.1.call-done = f32[8,768,384]{2,1,0:T(8,128)} async-done(((f32[1,768,384]{2,1,0:T(8,128)}), f32[8,768,384]{2,1,0:T(8,128)}) %all-gather.14.cloned.1.call-update) | async-done | bytes 9437200 | tf_op jit(solution)/shard_map/all_gather | solution.py:10
  499.4 4.3 reduce_sum.58
  503.6 5.9 scatter_fusion.2
  509.6 3.5 fusion.13
  513.1 0.3 conditional.5
  513.1 0.1 broadcast.1740
  513.4 1.1 broadcast_select_fusion
  514.5 0.0 all-gather.20.cloned.1.call-update
  514.5 123.9 %all-gather.20.cloned.1.call-done = f32[12288,384]{0,1:T(8,128)} async-done(((f32[768,384]{0,1:T(8,128)}), f32[12288,384]{0,1:T(8,128)}) %all-gather.20.cloned.1.call-update) | async-done | bytes 18874384 | tf_op jit(solution)/shard_map/all_gather | solution.py:16
  638.5 12.1 %copy.10 = f32[48,8,16,768]{3,2,1,0:T(8,128)S(1)} copy(f32[48,8,16,768]{3,1,2,0:T(8,128)} %bitcast.79) | data formatting | bytes 37748736
  650.6 3.2 bitcast_reduce_fusion
  653.8 0.4 copy.7
  654.2 4.5 fusion.12
  (35 shorter events, 0.2 us)
Async XLA Ops:
  6.5 1.3 copy-start.7
  6.5 62.7 %all-gather.10.cloned.1.call-start = ((), (), s32[]{:S(2)}) async-start(), calls=%async_computation | async-start | bytes 10616832 | tf_op jit(solution)/shard_map/all_gather | solution.py:10
  12.5 193.9 %all-gather.16.cloned.1.call-start = ((), (), s32[]{:S(2)}) async-start(), calls=%async_computation.3 | async-start | bytes 20054016 | tf_op jit(solution)/shard_map/all_gather | solution.py:16
  12.9 69.8 %copy-start = (pred[384,384]{1,0:T(32,128)(4,1)}, pred[384,384]{1,0:T(32,128)(4,1)S(1)}, u32[]{:S(2)}) copy-start(pred[384,384]{1,0:T(32,128)(4,1)S(1)} %iota_compare_fusion.4) | copy-start | bytes 442372
  87.8 196.3 %all-gather.12.cloned.1.call-start = ((), (), s32[]{:S(2)}) async-start(), calls=%async_computation.1 | async-start | bytes 10616832 | tf_op jit(solution)/shard_map/all_gather | solution.py:10
  227.0 2.2 copy-start.5
  230.3 191.3 %all-gather.18.cloned.1.call-start = ((), (), s32[]{:S(2)}) async-start(), calls=%async_computation.4 | async-start | bytes 20054016 | tf_op jit(solution)/shard_map/all_gather | solution.py:16
  294.2 3.5 copy-start.1
  299.0 0.7 copy-start.4
  299.0 1.3 copy-start.3
  299.1 200.3 %all-gather.14.cloned.1.call-start = ((), (), s32[]{:S(2)}) async-start(), calls=%async_computation.2 | async-start | bytes 10616832 | tf_op jit(solution)/shard_map/all_gather | solution.py:10
  442.1 2.2 copy-start.6
  445.5 192.9 %all-gather.20.cloned.1.call-start = ((), (), s32[]{:S(2)}) async-start(), calls=%async_computation.5 | async-start | bytes 20054016 | tf_op jit(solution)/shard_map/all_gather | solution.py:16
  509.6 3.5 copy-start.2
Sparse Core Ops, SparseCore 0:
  12.7 56.5 all-gather.9
  88.0 118.4 all-gather.15
  230.5 53.6 all-gather.11
  299.2 122.3 all-gather.17
  445.6 53.6 all-gather.13
  514.6 123.7 all-gather.19
